TPU v7x, 256 devices: a whole 4x4x8 slice. The times are simulated.
256 devices in a mesh: blk: 16 (over y_hi, z), rows: 16 (over x, y_lo, core).
Axes of the slice: x: 4, y: 4 (y_hi: 2, y_lo: 2; y = y_hi * 2 + y_lo), z: 8, core: 2. Of those that a mesh axis runs over, the one named last changes fastest.
Arguments:
- operator: float32 [16384, 16384], P('rows', 'blk'), may hold values from -60 to 60
Outputs:
- rotated: float32 [16384, 16384], P('rows', 'blk')
All inputs are finite; a program needn't handle non-finite values.
Results may differ from a plain program's by a relative error of at most 0.0001.
Values sent between devices are 32-bit elements; how exact they have to be, the bound alone decides.
A program may use at most 64 MiB of HBM per device.

v0:
```python
import jax
import jax.numpy as jnp
from jax import lax
from jax.sharding import PartitionSpec as P

BW = 256
ROUNDS = 2


HIGH = lax.Precision.HIGHEST


def shifted(value, axis, steps):
    count = lax.axis_size(axis)
    leading, last = (max(0, -steps), min(count, count - steps))
    return lax.ppermute(value, axis, [(source, source + steps) for source in range(leading, last)])


def rotation(coupling, upper_squares, lower_squares):
    width = coupling.shape[0]
    mixing = -coupling / (upper_squares[:, None] + lower_squares[None, :] + 1e-06)
    factor = jnp.sqrt(1.0 + jnp.sum(mixing * mixing))
    eye = jnp.eye(width, dtype=jnp.float32)
    top_row = jnp.concatenate([eye, mixing], axis=1)
    bottom_row = jnp.concatenate([-mixing.T, eye], axis=1)
    ortho = jnp.concatenate([top_row, bottom_row], axis=0) / factor
    square = jnp.dot(ortho.T, ortho, precision=HIGH, preferred_element_type=jnp.float32)
    ortho = 1.5 * ortho - 0.5 * jnp.dot(
        ortho, square, precision=HIGH, preferred_element_type=jnp.float32
    )
    return ortho


def local(operator):
    width = BW
    pairs = operator.shape[1] // (2 * width)
    uppers = [operator[:, 2 * slot * width : (2 * slot + 1) * width] for slot in range(pairs)]
    lowers = [operator[:, (2 * slot + 1) * width : (2 * slot + 2) * width] for slot in range(pairs)]
    position = lax.axis_index("blk")
    last_slot = lax.axis_size("blk") - 1
    for sweep in range(ROUNDS):
        paired = [jnp.concatenate([uppers[slot], lowers[slot]], axis=1) for slot in range(pairs)]
        local_gram = jnp.stack(
            [
                jnp.einsum(
                    "ra,rb->ab",
                    paired[slot],
                    paired[slot],
                    precision=HIGH,
                    preferred_element_type=jnp.float32,
                )
                for slot in range(pairs)
            ],
            axis=0,
        )
        gram = lax.psum(local_gram, "rows")
        couplings = [gram[slot, :width, width:] for slot in range(pairs)]
        squares = [jnp.diagonal(gram[slot]) for slot in range(pairs)]
        for slot in range(pairs):
            ortho = rotation(couplings[slot], squares[slot][:width], squares[slot][width:])
            turned = jnp.dot(
                paired[slot], ortho, precision=HIGH, preferred_element_type=jnp.float32
            )
            uppers[slot] = turned[:, :width]
            lowers[slot] = turned[:, width:]
        if sweep + 1 < ROUNDS:
            incoming_upper = shifted(uppers[pairs - 1], "blk", 1)
            incoming_lower = shifted(lowers[0], "blk", -1)
            new_uppers = [jnp.where(position == 0, uppers[0], incoming_upper)]
            slot = 1
            new_uppers.append(jnp.where(position == 0, lowers[0], uppers[0]))
            new_lowers = [lowers[1]]
            new_lowers.append(jnp.where(position == last_slot, uppers[pairs - 1], incoming_lower))
            uppers, lowers = (new_uppers, new_lowers)
    pieces = []
    for slot in range(pairs):
        pieces.append(uppers[slot])
        pieces.append(lowers[slot])
    return jnp.concatenate(pieces, axis=1)


def solution(mesh):
    placed = (P("rows", "blk"),)
    return jax.shard_map(
        local, mesh=mesh, in_specs=placed, out_specs=P("rows", "blk"), check_vma=False
    )
```

profile of v0, /device:TPU:1, one launch (start us, length us, event | category | flops | bytes accessed | tf_op | source)
XLA Modules:
  0.0 411.6 jit_solution(591069598848751240)
XLA Ops:
  6.5 5.7 %fusion.23 = f32[1,512,512]{2,1,0:T(8,128)S(1)} fusion(f32[1024,1024]{1,0:T(8,128)} %param.1), kind=kOutput, calls=%fused_computation.32 | convolution fusion | flops 3221225472 | bytes 3145728 | tf_op jit(solution)/shard_map/ra,rb->ab/dot_general | solution.py:45
  12.2 5.7 %fusion.20 = f32[1,512,512]{2,1,0:T(8,128)S(1)} fusion(f32[1024,1024]{1,0:T(8,128)} %param.1), kind=kOutput, calls=%fused_computation.31 | convolution fusion | flops 3221225472 | bytes 3145728 | tf_op jit(solution)/shard_map/ra,rb->ab/dot_general | solution.py:45
  18.0 1.5 pad_maximum_fusion.1
  19.5 0.2 all-reduce.5.cloned.1.call-start
  19.7 0.8 copy.16
  20.6 131.1 %all-reduce.3.cloned.1.call-done = f32[2,512,512]{2,1,0:T(8,128)} async-done(((f32[2,512,512]{2,1,0:T(8,128)}), f32[2,512,512]{2,1,0:T(8,128)}) %all-reduce.3.cloned.1.call-update) | async-done | bytes 2097168 | tf_op jit(solution)/shard_map/psum | solution.py:56
  151.7 1.7 slice_bitcast_fusion.2
  153.4 4.5 %gather_fusion.1 = f32[512]{0:T(512)S(1)} fusion(f32[512,512]{1,0:T(8,128)S(1)} %get-tuple-element.22, s32[512]{0:T(512)S(1)} %bitcast.55), kind=kCustom, calls=%fused_computation.1 | custom fusion | bytes 8192 | tf_op jit(solution)/shard_map/jit(diagonal)/cond/branch_0_fun/gather | solution.py:58
  158.0 0.1 copy.21
  158.2 1.6 multiply_reduce_fusion.2
  159.8 0.1 copy.22
  160.0 1.0 slice.100
  160.9 0.1 copy.30
  161.1 4.5 %gather_fusion = f32[512]{0:T(512)S(1)} fusion(f32[512,512]{1,0:T(8,128)S(1)} %get-tuple-element.23, s32[512]{0:T(512)S(1)} %bitcast.56), kind=kCustom, calls=%fused_computation | custom fusion | bytes 8192 | tf_op jit(solution)/shard_map/jit(diagonal)/cond/branch_0_fun/gather | solution.py:58
  166.3 1.9 fusion.50
  168.2 1.9 fusion.28
  170.2 0.2 copy-done.3
  170.4 3.6 fusion.15
  174.0 1.5 fusion.68
  175.4 4.3 %collective-permute-start = (f32[1024,256]{0,1:T(8,128)}, f32[1024,256]{0,1:T(8,128)}, u32[]{:S(2)}, u32[]{:S(2)}) collective-permute-start(f32[1024,256]{0,1:T(8,128)} %get-tuple-element.20), channel_id=1, source_target_pairs={{0,16},{16,32},{32,48},{48,64},{64,80},{80,96},{96,112},{112,128},... | collective-permute-start | bytes 3145736 | tf_op jit(solution)/shard_map/ppermute | solution.py:16
  179.7 0.8 multiply_reduce_fusion.3
  180.5 0.1 copy.17
  181.4 1.9 fusion.43
  183.3 3.1 fusion.29
  186.4 6.9 %fusion.12 = f32[1024,512]{0,1:T(8,128)S(1)} fusion(f32[512,512]{1,0:T(8,128)S(1)} %fusion.29, f32[1024,1024]{1,0:T(8,128)S(1)} %copy-done.4), kind=kOutput, calls=%fused_computation.27 | convolution fusion | flops 3221225472 | bytes 5242880 | tf_op jit(solution)/shard_map/dot_general | solution.py:61
  193.4 6.6 %collective-permute-done = f32[1024,256]{0,1:T(8,128)} collective-permute-done((f32[1024,256]{0,1:T(8,128)}, f32[1024,256]{0,1:T(8,128)}, u32[]{:S(2)}, u32[]{:S(2)}) %collective-permute-start) | collective-permute-done | bytes 1048608 | tf_op jit(solution)/shard_map/ppermute | solution.py:16
  200.0 1.8 slice_select_fusion.1
  201.8 1.7 collective-permute-start.1
  203.5 5.7 %fusion.18 = f32[1,512,512]{1,2,0:T(8,128)S(1)} fusion(f32[1024,256]{0,1:T(8,128)} %get-tuple-element.21, f32[1024,256]{0,1:T(8,128)} %get-tuple-element.17), kind=kOutput, calls=%fused_computation.29 | convolution fusion | flops 3221749760 | bytes 3145728 | tf_op jit(solution)/shard_map/ra,rb->ab/dot_general | solution.py:45
  209.2 19.5 %collective-permute-done.1 = f32[1024,256]{0,1:T(8,128)} collective-permute-done((f32[1024,256]{0,1:T(8,128)}, f32[1024,256]{0,1:T(8,128)}, u32[]{:S(2)}, u32[]{:S(2)}) %collective-permute-start.1) | collective-permute-done | bytes 1048608 | tf_op jit(solution)/shard_map/ppermute | solution.py:16
  228.7 1.4 broadcast_select_fusion
  230.1 1.0 copy-done.1
  231.1 3.6 fusion.19
  234.7 1.5 pad_maximum_fusion.4
  236.2 130.9 %all-reduce.5.cloned.1.call-done = f32[2,512,512]{1,2,0:T(8,128)} async-done(((f32[2,512,512]{1,2,0:T(8,128)}), f32[2,512,512]{1,2,0:T(8,128)}) %all-reduce.5.cloned.1.call-update) | async-done | bytes 2097168 | tf_op jit(solution)/shard_map/psum | solution.py:56
  367.1 1.7 slice_bitcast_fusion.1
  368.8 4.5 %gather_fusion.2 = f32[512]{0:T(512)S(1)} fusion(f32[512,512]{0,1:T(8,128)S(1)} %get-tuple-element.15, s32[512]{0:T(512)S(1)} %bitcast.57), kind=kCustom, calls=%fused_computation.2 | custom fusion | bytes 8192 | tf_op jit(solution)/shard_map/jit(diagonal)/cond/branch_0_fun/gather | solution.py:58
  373.3 4.7 %gather_fusion.3 = f32[512]{0:T(512)S(1)} fusion(f32[512,512]{0,1:T(8,128)S(1)} %get-tuple-element.16, s32[512]{0:T(512)S(1)} %bitcast.58), kind=kCustom, calls=%fused_computation.3 | custom fusion | bytes 8192 | tf_op jit(solution)/shard_map/jit(diagonal)/cond/branch_0_fun/gather | solution.py:58
  378.1 1.9 multiply_reduce_fusion.1
  381.4 0.1 copy.26
  381.7 1.9 fusion.47
  383.6 2.0 fusion.27
  385.6 3.5 fusion.10
  389.1 1.9 fusion.44
  391.0 2.0 fusion.26
  393.0 3.8 fusion.8
  396.7 2.5 pad_maximum_fusion
  399.2 5.3 %copy.27 = f32[1024,1024]{1,0:T(8,128)} copy(f32[1024,1024]{0,1:T(8,128)} %pad_maximum_fusion) | data formatting | bytes 8388608 | tf_op jit(solution)/shard_map/concatenate | solution.py:79
  (34 shorter events, 0.5 us)
Async XLA Ops:
  6.5 145.1 %all-reduce.3.cloned.1.call-start = ((), (), s32[]{:S(2)}) async-start(), calls=%async_computation | async-start | bytes 4194304 | tf_op jit(solution)/shard_map/psum | solution.py:56
  19.5 347.6 %all-reduce.5.cloned.1.call-start = ((), (), s32[]{:S(2)}) async-start(), calls=%async_computation.1 | async-start | bytes 4194304 | tf_op jit(solution)/shard_map/psum | solution.py:56
  19.7 148.5 %copy-start.6 = (f32[256,256]{0,1:T(8,128)}, f32[256,256]{0,1:T(8,128)S(1)}, u32[]{:S(2)}) copy-start(f32[256,256]{0,1:T(8,128)S(1)} %fusion.42) | copy-start | bytes 786436
  168.2 2.2 copy-start.3
  174.0 7.4 %copy-start.8 = (f32[256,256]{1,0:T(8,128)S(1)}, f32[256,256]{1,0:T(8,128)}, u32[]{:S(2)}) copy-start(f32[256,256]{1,0:T(8,128)} %copy.16) | copy-start | bytes 786436
  175.4 24.6 %collective-permute-start = (f32[1024,256]{0,1:T(8,128)}, f32[1024,256]{0,1:T(8,128)}, u32[]{:S(2)}, u32[]{:S(2)}) collective-permute-start(f32[1024,256]{0,1:T(8,128)} %get-tuple-element.20), channel_id=1, source_target_pairs={{0,16},{16,32},{32,48},{48,64},{64,80},{80,96},{96,112},{112,128},... | collective-permute-start | bytes 3145736 | tf_op jit(solution)/shard_map/ppermute | solution.py:16
  180.6 0.7 copy-start.10
  181.4 1.9 copy-start.9
  183.3 3.1 copy-start.4
  201.8 26.9 %collective-permute-start.1 = (f32[1024,256]{0,1:T(8,128)}, f32[1024,256]{0,1:T(8,128)}, u32[]{:S(2)}, u32[]{:S(2)}) collective-permute-start(f32[1024,256]{0,1:T(8,128)} %get-tuple-element.19), channel_id=1, source_target_pairs={{16,0},{32,16},{48,32},{64,48},{80,64},{96,80},{112,96},{128,112},... | collective-permute-start | bytes 3145736 | tf_op jit(solution)/shard_map/ppermute | solution.py:16
  230.1 1.0 copy-start.1
  378.1 3.6 copy-start.7
  383.6 2.0 copy-start
  383.6 2.0 copy-start.5
  391.0 2.0 copy-start.2
Sparse Core Ops, SparseCore 0:
  19.6 132.0 all-reduce.2
  236.3 130.7 all-reduce.4
where the time goes:
time: 418 us; the launch traced here: 412 us
  waiting for transfers between devices  288 us (69%)
  matrix products  54.9 us (13%)
  local copies, waits for them, and re-layouts  32.5 us (8%)
  between operations  16.7 us (4%)
  other arithmetic  13.2 us (3%)
  starting transfers between devices  6.18 us (1%)
    psum x2, waiting for transfers between devices, local(): gram = lax.psum(local_gram, 'rows')  262 us
    ppermute x2, waiting for transfers between devices, shifted(): lax.ppermute(value, axis, [(source, source + steps) for source in range(l...  26.1 us
    dot_general x4, matrix products, local(): jnp.einsum('ra,rb->ab', paired[slot], paired[slot], precision=HIGH, prefe...  20.6 us
    gather x4, local copies, waits for them, and re-layouts, local(): squares = [jnp.diagonal(gram[slot]) for slot in range(pairs)]  18.3 us
    dot_general x4, matrix products, local(): jnp.dot(paired[slot], ortho, precision=HIGH, preferred_element_type=jnp.f...  17.8 us
    dot_general x4, matrix products, rotation(): jnp.dot(ortho, square, precision=HIGH, preferred_element_type=jnp.float32)  8.98 us
  transfers between devices with their start and end apart: 4, of which 4 were waited for; matrix products, arithmetic and copies ran while one was open for 5% of the time, Pallas kernels for 0%

commit v1 on v0

v1 whole, which is shorter than its diff:
```python
import functools

import jax
import jax.numpy as jnp
from jax import lax
from jax.experimental import pallas as pl
from jax.experimental.pallas import tpu as pltpu
from jax.sharding import PartitionSpec as P

BW = 256
HB = 128
MESH = pl.DeviceIdType.MESH
F32 = jnp.float32
BF16 = jnp.bfloat16
FAR = (5, 4, 3, 7, 1, 2, 6)


def dot(a, b, contract):
    return lax.dot_general(a, b, (contract, ((), ())), preferred_element_type=F32)


NN = ((1,), (0,))
NT = ((1,), (1,))
TN = ((0,), (0,))


def split(value):
    high = value.astype(BF16)
    return high, (value - high.astype(F32)).astype(BF16)


def eye(rows, columns):
    return lax.broadcasted_iota(jnp.int32, (rows, columns), 0) == lax.broadcasted_iota(
        jnp.int32, (rows, columns), 1
    )


def write_rotation(x, w_ref):
    xh, xl = split(x)
    total = jnp.sum(jnp.sum(x * x, axis=0, keepdims=True), axis=1, keepdims=True)
    inv = 1.0 / jnp.sqrt(1.0 + total)
    b = 0.5 * inv * inv * inv
    a = 1.5 * inv - b
    left = dot(
        jnp.concatenate([xh, xl, xh], axis=1), jnp.concatenate([xh, xh, xl], axis=1), NT
    )
    right = dot(
        jnp.concatenate([xh, xl, xh], axis=0), jnp.concatenate([xh, xh, xl], axis=0), TN
    )
    lh, ll = split(left)
    cube = dot(
        jnp.concatenate([lh, ll, lh], axis=1), jnp.concatenate([xh, xh, xl], axis=0), NN
    )
    z = a * x - b * cube
    diagonal = jnp.where(eye(BW, BW), jnp.broadcast_to(a, (BW, BW)), 0.0)
    parts = (
        (0, 0, diagonal - b * left),
        (0, BW, z),
        (BW, 0, -z.T),
        (BW, BW, diagonal - b * right),
    )
    for row, column, value in parts:
        high, low = split(value)
        w_ref[row : row + BW, column : column + BW] = high
        w_ref[2 * BW + row : 3 * BW + row, column : column + BW] = low


def turn(hl, w_ref, column):
    wh = w_ref[0 : 2 * BW, column : column + BW]
    wl = w_ref[2 * BW : 4 * BW, column : column + BW]
    return dot(
        jnp.concatenate([hl, hl[:, : 2 * BW]], axis=1),
        jnp.concatenate([wh, wh, wl], axis=0),
        NN,
    )


def gram(ah, al, bh, bl):
    both = dot(ah, jnp.concatenate([bh, bl], axis=1), TN)
    return both[:, :BW] + both[:, BW:] + dot(al, bh, TN)


def pack(ts, slot, t, g, h):
    size = t.shape[0] // 4
    line = lax.broadcasted_iota(jnp.int32, (8, HB), 0)
    for j in range(8):
        half, quarter = j // 4, j % 4
        ts[slot, j, 0:size, :] = t[quarter * size : (quarter + 1) * size, half * HB : (half + 1) * HB]
        start = quarter * size
        wide = jnp.broadcast_to(g[:, start // HB * HB : start // HB * HB + HB], (8, HB))
        if start % HB:
            wide = pltpu.roll(wide, HB - start % HB, 1)
        lower = jnp.broadcast_to(h[:, half * HB : (half + 1) * HB], (8, HB))
        ts[slot, j, size : size + 8, :] = jnp.where(line == 0, wide, lower)


def jacobi(
    op, hl_out, x_out,
    pin, hl1, hl2, w, sb, ra, rl, hsum,
    ts0, ts1, ts2, tr0, tr1, tr2, rs0, rs1, rs2, rd0, rd1, rd2, xb0, xb1, xb2,
    load_sem, out_sem, core_send, core_recv, rs_send, rs_recv, ag_send, ag_recv,
    fw_send, fw_recv, z_send, z_recv, rl_send, rl_recv,
):
    blk = lax.axis_index("blk")
    rows = lax.axis_index("rows")
    blocks = lax.axis_size("blk")
    last = blocks - 1
    middle = blocks // 2
    is_relay = (blk == 0) | (blk == last)
    is_middle = (blk == middle - 1) | (blk == middle)
    core = rows % 2
    chip = rows // 2
    px, py = rows // 4, chip % 2
    sibling = (blk, chip * 2 + 1 - core)
    other = 1 - core
    slots = (other, core)

    def mate(k):
        return ((px + k // 2) % 4) * 2 + (py + k % 2) % 2

    def source(k):
        return ((px + 4 - k // 2) % 4) * 2 + (py + k % 2) % 2

    loads = {}
    for i, slot in enumerate(slots):
        shift = jnp.where((slot == 0) & (blk > 0), BW, 0)
        for part, column in enumerate((slot * 2 * BW + shift, slot * 2 * BW + BW - shift)):
            loads[i, part] = pltpu.make_async_copy(
                op.at[:, pl.ds(pl.multiple_of(column, BW), BW)],
                pin.at[slot, part],
                load_sem.at[slot, part],
            )
            loads[i, part].start()

    barrier = pltpu.get_barrier_semaphore()
    pl.semaphore_signal(barrier, inc=1, device_id=sibling, device_id_type=MESH)
    for k in FAR:
        pl.semaphore_signal(
            barrier, inc=1, device_id=(blk, mate(k) * 2 + core), device_id_type=MESH
        )

    @pl.when(blk > 0)
    def _():
        pl.semaphore_signal(barrier, inc=1, device_id=(blk - 1, rows), device_id_type=MESH)

    @pl.when(blk < last)
    def _():
        pl.semaphore_signal(barrier, inc=1, device_id=(blk + 1, rows), device_id_type=MESH)

    @pl.when(is_relay)
    def _():
        for side in range(2):
            pl.semaphore_signal(
                barrier, inc=1, device_id=(middle - side, rows), device_id_type=MESH
            )

    @pl.when(is_middle)
    def _():
        for end in (0, last):
            pl.semaphore_signal(barrier, inc=1, device_id=(end, rows), device_id_type=MESH)

    greetings = 8 + jnp.where(blk > 0, 1, 0) + jnp.where(blk < last, 1, 0)
    greetings = greetings + jnp.where(is_relay | is_middle, 2, 0)
    pending = []

    def remote(src, dst, send, recv, target):
        return pltpu.make_async_remote_copy(
            src_ref=src, dst_ref=dst, send_sem=send, recv_sem=recv,
            device_id=target, device_id_type=MESH,
        )

    def core_copy(i, ts, tr):
        return remote(ts.at[other], tr, core_send.at[i], core_recv.at[i], sibling)

    def reduce_own(i, ts, tr, rs, rd, xb, sign):
        size = rs.shape[1] - 8
        core_copy(i, ts, tr).wait_recv()
        for k in FAR:
            rs[mate(k)] = ts[core, mate(k)] + tr[mate(k)]
            copy = remote(
                rs.at[mate(k)], rd.at[k], rs_send.at[i, k], rs_recv.at[i, k],
                (blk, mate(k) * 2 + core),
            )
            copy.start()
            pending.append(copy)
        total = ts[core, chip] + tr[chip]
        for k in FAR[::-1]:
            remote(
                rs.at[mate(k)], rd.at[k], rs_send.at[i, k], rs_recv.at[i, k],
                (blk, mate(k) * 2 + core),
            ).wait_recv()
            total = total + rd[k]
        g = jnp.sum(
            jnp.where(eye(size, HB), jnp.broadcast_to(total[size : size + 1], (size, HB)), 0.0),
            axis=1, keepdims=True,
        )
        h = total[size + 1 : size + 2]
        xb[core, chip] = sign * total[:size] / (g + h + 1e-06)
        for k in FAR:
            copy = remote(
                xb.at[core, chip], xb.at[core, chip], ag_send.at[i, k], ag_recv.at[i, k],
                (blk, mate(k) * 2 + core),
            )
            copy.start()
            pending.append(copy)
        copy = remote(
            xb.at[core, chip], xb.at[core, chip], fw_send.at[i, 0], fw_recv.at[i, 0], sibling
        )
        copy.start()
        pending.append(copy)

    def hand_on(i, xb):
        for k in FAR[::-1]:
            piece = xb.at[core, source(k)]
            remote(
                piece, piece, ag_send.at[i, k], ag_recv.at[i, k], (blk, mate(k) * 2 + core)
            ).wait_recv()
            copy = remote(piece, piece, fw_send.at[i, k], fw_recv.at[i, k], sibling)
            copy.start()
            pending.append(copy)

    def receive_other(i, xb):
        for k in (0,) + FAR[::-1]:
            piece = xb.at[other, source(k)]
            remote(piece, piece, fw_send.at[i, k], fw_recv.at[i, k], sibling).wait_recv()

    for i, slot in enumerate(slots):
        loads[i, 0].wait()
        loads[i, 1].wait()

        def part(n, sums, slot=slot):
            at = pl.ds(pl.multiple_of(n * HB, HB), HB)
            out = []
            for p in range(2):
                value = pin[slot, p, at, :]
                high, low = split(value)
                hl1[slot, at, p * BW : (p + 1) * BW] = high
                hl1[slot, at, (2 + p) * BW : (3 + p) * BW] = low
                out.append(sums[p] + jnp.sum(value * value, axis=0, keepdims=True))
            return tuple(out)

        zero = jnp.zeros((1, BW), F32)
        g, h = lax.fori_loop(0, pin.shape[2] // HB, part, (zero, zero))
        t = gram(
            hl1[slot, :, 0:BW], hl1[slot, :, 2 * BW : 3 * BW],
            hl1[slot, :, BW : 2 * BW], hl1[slot, :, 3 * BW : 4 * BW],
        )
        pack(ts0, slot, t, g, h)
        if i == 0:
            pl.semaphore_wait(barrier, greetings)
            copy = core_copy(0, ts0, tr0)
            copy.start()
            pending.append(copy)
    sign = jnp.where((core == 0) & (blk > 0), 1.0, -1.0)
    reduce_own(0, ts0, tr0, rs0, rd0, xb0, sign)
    hand_on(0, xb0)

    half_rows = pin.shape[2] // 2

    def z_away(slot, column, m):
        at = pl.ds(m * half_rows, half_rows)
        return remote(
            sb.at[slot, column, at], ra.at[1 - slot, column, at],
            z_send.at[slot, column, m], z_recv.at[1 - slot, column, m],
            (jnp.clip(blk + 2 * slot - 1, 0, last), rows),
        )

    def z_here(slot, column, m):
        at = pl.ds(m * half_rows, half_rows)
        return pltpu.make_async_copy(
            sb.at[slot, column, at], ra.at[slot, column, at], z_recv.at[slot, column, m]
        )

    def at_edge(slot):
        return blk == slot * last

    def z_start(slot, column, m):
        @pl.when(at_edge(slot))
        def _():
            z_here(slot, column, m).start()

        if m == 0:

            @pl.when(jnp.logical_not(at_edge(slot)))
            def _():
                z_away(slot, column, m).start()

        else:

            @pl.when(jnp.logical_not(at_edge(slot) | (blk == middle - slot)))
            def _():
                z_away(slot, column, m).start()

            @pl.when(blk == middle - slot)
            def _():
                remote(
                    sb.at[slot, column, pl.ds(half_rows, half_rows)], rl.at[column],
                    z_send.at[slot, column, 1], rl_recv.at[column], (last * slot, rows),
                ).start()

    def relay(column):
        goal = jnp.where(blk == last, 0, 1)
        return remote(
            rl.at[column], ra.at[goal, column, pl.ds(half_rows, half_rows)],
            rl_send.at[column], z_recv.at[goal, column, 1], (middle - goal, rows),
        )

    def pass_on(column):
        @pl.when(is_relay)
        def _():
            remote(
                rl.at[column], rl.at[column], rl_send.at[column], rl_recv.at[column], sibling
            ).wait_recv()
            relay(column).start()

    def z_wait_recv(slot, column, m):
        at = pl.ds(m * half_rows, half_rows)

        @pl.when(at_edge(slot))
        def _():
            z_here(slot, column, m).wait()

        @pl.when(jnp.logical_not(at_edge(slot)))
        def _():
            remote(
                sb.at[slot, column, at], ra.at[slot, column, at],
                z_send.at[slot, column, m], z_recv.at[slot, column, m], sibling,
            ).wait_recv()

    for i, slot in enumerate((core, other)):
        if i == 1:
            receive_other(0, xb0)
        x = jnp.concatenate(
            [jnp.concatenate([xb0[slot, 4 * p + n] for n in range(4)], axis=0) for p in range(2)],
            axis=1,
        )
        write_rotation(x, w.at[slot])
        for m in range(2):
            at = pl.ds(m * half_rows, half_rows)
            moved = turn(hl1[slot, at, :], w.at[slot], 0)
            sb[slot, 0, at, :] = moved[:, :HB]
            z_start(slot, 0, m)
            sb[slot, 1, at, :] = moved[:, HB:]
    for slot in (core, other):
        for m in range(2):
            z_start(slot, 1, m)
    for slot in (core, other):
        h = jnp.zeros((1, BW), F32)
        for m in range(2):
            at = pl.ds(m * half_rows, half_rows)
            kept = turn(hl1[slot, at, :], w.at[slot], BW)
            high, low = split(kept)
            hl2[1 - slot, at, BW : 2 * BW] = high
            hl2[1 - slot, at, 3 * BW : 4 * BW] = low
            h = h + jnp.sum(kept * kept, axis=0, keepdims=True)
        hsum[1 - slot] = jnp.broadcast_to(h, (8, BW))

    pass_on(0)
    sign = jnp.where(core == 0, -1.0, 1.0)
    second = ((ts1, tr1, rs1, rd1, xb1), (ts2, tr2, rs2, rd2, xb2))
    for column, (ts, tr, rs, rd, xb) in enumerate(second):
        for i, slot in enumerate(slots):
            for m in range(2):
                z_wait_recv(slot, column, m)

            def part(n, g, slot=slot, column=column):
                at = pl.ds(pl.multiple_of(n * HB, HB), HB)
                value = ra[slot, column, at, :]
                high, low = split(value)
                hl2[slot, at, column * HB : (column + 1) * HB] = high
                hl2[slot, at, 2 * BW + column * HB : 2 * BW + (column + 1) * HB] = low
                return g + jnp.sum(value * value, axis=0, keepdims=True)

            g = lax.fori_loop(0, pin.shape[2] // HB, part, jnp.zeros((1, HB), F32))
            t = gram(
                hl2[slot, :, column * HB : (column + 1) * HB],
                hl2[slot, :, 2 * BW + column * HB : 2 * BW + (column + 1) * HB],
                hl2[slot, :, BW : 2 * BW], hl2[slot, :, 3 * BW : 4 * BW],
            )
            pack(ts, slot, t, g, hsum[slot, 0:1, :])
            if i == 0:
                copy = core_copy(1 + column, ts, tr)
                copy.start()
                pending.append(copy)
        if column == 0:
            pass_on(1)
        if column == 1:
            whole = pltpu.make_async_copy(hl2, hl_out, out_sem.at[0])
            whole.start()
            hand_on(1, xb1)
        reduce_own(1 + column, ts, tr, rs, rd, xb, sign)
    hand_on(2, xb2)
    outs = []
    for column, xb in enumerate((xb1, xb2)):
        receive_other(1 + column, xb)
        copy = pltpu.make_async_copy(xb, x_out.at[column], out_sem.at[1 + column])
        copy.start()
        outs.append(copy)
    for copy in pending:
        copy.wait_send()
    for slot in range(2):
        for column in range(2):
            for m in range(2):

                @pl.when(jnp.logical_not(at_edge(slot)))
                def _():
                    z_away(slot, column, m).wait_send()

    @pl.when(is_relay)
    def _():
        for column in range(2):
            relay(column).wait_send()

    whole.wait()
    for copy in outs:
        copy.wait()


def finish(hl_in, x_in, out, hl, xv, w, ob, hl_sem, x_sem, out_sem):
    count = 2
    size = hl.shape[1] // count
    x_copy = pltpu.make_async_copy(x_in, xv, x_sem)
    x_copy.start()
    loads = {}
    for slot in range(2):
        for m in range(count):
            at = pl.ds(m * size, size)
            loads[slot, m] = pltpu.make_async_copy(
                hl_in.at[slot, at], hl.at[slot, at], hl_sem.at[slot, m]
            )
            loads[slot, m].start()
    x_copy.wait()
    stores = []
    for slot in range(2):
        x = jnp.concatenate(
            [
                jnp.concatenate(
                    [xv[column, slot, 4 * p + n] for column in range(2) for n in range(4)], axis=0
                )
                for p in range(2)
            ],
            axis=1,
        )
        write_rotation(x, w.at[slot])
        for m in range(count):
            at = pl.ds(m * size, size)
            loads[slot, m].wait()
            lhs = hl[slot, at, :]
            first = slot * 2 * BW
            for p in range(2):
                column = first + (p * BW if slot == 0 else BW - p * BW)
                ob[at, column : column + BW] = turn(lhs, w.at[slot], p * BW)
            copy = pltpu.make_async_copy(
                ob.at[at, pl.ds(first, 2 * BW)],
                out.at[at, pl.ds(first, 2 * BW)],
                out_sem.at[slot, m],
            )
            copy.start()
            stores.append(copy)
    for copy in stores:
        copy.wait()


def local(operator):
    rows = operator.shape[0]
    any_spec = pl.BlockSpec(memory_space=pl.ANY)
    dma = pltpu.SemaphoreType.DMA

    def per_step(make):
        return [make(64), make(32), make(32)]

    hl, x = pl.pallas_call(
        jacobi,
        out_shape=(
            jax.ShapeDtypeStruct((2, rows, 4 * BW), BF16),
            jax.ShapeDtypeStruct((2, 2, 8, 32, HB), F32),
        ),
        in_specs=[any_spec],
        out_specs=(any_spec, any_spec),
        scratch_shapes=[
            pltpu.VMEM((2, 2, rows, BW), F32),
            pltpu.VMEM((2, rows, 4 * BW), BF16),
            pltpu.VMEM((2, rows, 4 * BW), BF16),
            pltpu.VMEM((2, 4 * BW, 2 * BW), BF16),
            pltpu.VMEM((2, 2, rows, HB), F32),
            pltpu.VMEM((2, 2, rows, HB), F32),
            pltpu.VMEM((2, rows // 2, HB), F32),
            pltpu.VMEM((2, 8, BW), F32),
            *per_step(lambda size: pltpu.VMEM((2, 8, size + 8, HB), F32)),
            *per_step(lambda size: pltpu.VMEM((8, size + 8, HB), F32)),
            *per_step(lambda size: pltpu.VMEM((8, size + 8, HB), F32)),
            *per_step(lambda size: pltpu.VMEM((8, size + 8, HB), F32)),
            *per_step(lambda size: pltpu.VMEM((2, 8, size, HB), F32)),
            dma((2, 2)),
            dma((3,)),
            dma((3,)),
            dma((3,)),
            dma((3, 8)),
            dma((3, 8)),
            dma((3, 8)),
            dma((3, 8)),
            dma((3, 8)),
            dma((3, 8)),
            dma((2, 2, 2)),
            dma((2, 2, 2)),
            dma((2,)),
            dma((2,)),
        ],
        compiler_params=pltpu.CompilerParams(
            collective_id=0, has_side_effects=True, vmem_limit_bytes=48 * 2**20
        ),
        name="jacobi",
    )(operator)
    return pl.pallas_call(
        finish,
        out_shape=jax.ShapeDtypeStruct(operator.shape, F32),
        in_specs=[any_spec, any_spec],
        out_specs=any_spec,
        scratch_shapes=[
            pltpu.VMEM((2, rows, 4 * BW), BF16),
            pltpu.VMEM((2, 2, 8, 32, HB), F32),
            pltpu.VMEM((2, 4 * BW, 2 * BW), BF16),
            pltpu.VMEM((rows, 4 * BW), F32),
            dma((2, 2)),
            dma,
            dma((2, 2)),
        ],
        compiler_params=pltpu.CompilerParams(vmem_limit_bytes=40 * 2**20),
        name="finish",
    )(hl, x)


def solution(mesh):
    placed = P("rows", "blk")
    return jax.shard_map(local, mesh=mesh, in_specs=(placed,), out_specs=placed, check_vma=False)
```

time: 418 us -> 68.7 us (0.16)
  the two profiles are of different devices: /device:TPU:1 before, /device:TPU:17 now
where the time goes in v1:
time: 68.7 us
  Pallas kernels  68.5 us (100%)
    pallas_call x1, Pallas kernels, local(): pl.pallas_call(jacobi, out_shape=(jax.ShapeDtypeStruct((2, rows, 4 * BW),...  61.9 us
    pallas_call x1, Pallas kernels, local(): pl.pallas_call(finish, out_shape=jax.ShapeDtypeStruct(operator.shape, F32...  6.61 us

profile of v1, /device:TPU:17, one launch (start us, length us, event | category | flops | bytes accessed | tf_op | source)
XLA Modules:
  0.0 68.7 jit_solution(11771018893016274725)
XLA Ops:
  0.0 61.9 %jacobi.1 = (bf16[2,1024,1024]{2,1,0:T(8,128)(2,1)S(1)}, f32[2,2,8,32,128]{4,3,2,1,0:T(8,128)S(1)}) custom-call(f32[1024,1024]{1,0:T(8,128)} %op.1), custom_call_target="tpu_custom_call" | custom-call | tf_op jit(solution)/shard_map/jacobi/pallas_call | solution.py:472
  61.9 6.6 %finish.1 = f32[1024,1024]{1,0:T(8,128)} custom-call(bf16[2,1024,1024]{2,1,0:T(8,128)(2,1)S(1)} %get-tuple-element.7.hl_in, f32[2,2,8,32,128]{4,3,2,1,0:T(8,128)S(1)} %get-tuple-element.8.x_in), custom_call_target="tpu_custom_call" | custom-call | tf_op jit(solution)/shard_map/finish/pallas_call | solution.py:514

commit v2 on v1

--- a/solution.py
+++ b/solution.py
@@ -96,10 +96,11 @@
 
 def jacobi(
     op, hl_out, x_out,
-    pin, hl1, hl2, w, sb, ra, rl, hsum,
+    pin, hl1, hl2, w, sb, ra, rl, raw, xn, hsum,
     ts0, ts1, ts2, tr0, tr1, tr2, rs0, rs1, rs2, rd0, rd1, rd2, xb0, xb1, xb2,
     load_sem, out_sem, core_send, core_recv, rs_send, rs_recv, ag_send, ag_recv,
     fw_send, fw_recv, z_send, z_recv, rl_send, rl_recv,
+    raw_send, raw_recv, xz_send, xz_recv,
 ):
     blk = lax.axis_index("blk")
     rows = lax.axis_index("rows")
@@ -108,9 +109,16 @@
     middle = blocks // 2
     is_relay = (blk == 0) | (blk == last)
     is_middle = (blk == middle - 1) | (blk == middle)
+    late = is_relay | is_middle
     core = rows % 2
     chip = rows // 2
     px, py = rows // 4, chip % 2
+    plain = pin.shape[2] - 256
+    sizes, kinds = (320, 320, 128, 256), (0, 0, 1, 2)
+    pieces = [(sum(sizes[:m]), sizes[m]) for m in range(len(sizes))]
+    direct = sum(size for size, kind in zip(sizes, kinds) if kind == 0)
+    count = len(sizes)
+    tail = pl.ds(plain, 256)
     sibling = (blk, chip * 2 + 1 - core)
     other = 1 - core
     slots = (other, core)
@@ -121,10 +129,25 @@
     def source(k):
         return ((px + 4 - k // 2) % 4) * 2 + (py + k % 2) % 2
 
+    def at_edge(slot):
+        return blk == slot * last
+
+    def crosses(slot):
+        return blk == middle - slot
+
+    def ahead(slot):
+        return jnp.logical_not(at_edge(slot) | crosses(slot))
+
+    def beside(slot):
+        return (jnp.clip(blk + 2 * slot - 1, 0, last), rows)
+
+    def columns(slot):
+        shift = jnp.where((slot == 0) & (blk > 0), BW, 0)
+        return slot * 2 * BW + shift, slot * 2 * BW + BW - shift
+
     loads = {}
     for i, slot in enumerate(slots):
-        shift = jnp.where((slot == 0) & (blk > 0), BW, 0)
-        for part, column in enumerate((slot * 2 * BW + shift, slot * 2 * BW + BW - shift)):
+        for part, column in enumerate(columns(slot)):
             loads[i, part] = pltpu.make_async_copy(
                 op.at[:, pl.ds(pl.multiple_of(column, BW), BW)],
                 pin.at[slot, part],
@@ -172,23 +195,59 @@
     def core_copy(i, ts, tr):
         return remote(ts.at[other], tr, core_send.at[i], core_recv.at[i], sibling)
 
-    def reduce_own(i, ts, tr, rs, rd, xb, sign):
-        size = rs.shape[1] - 8
+    def raw_copy(slot, part):
+        return remote(
+            op.at[pl.ds(plain, 256), pl.ds(pl.multiple_of(columns(slot)[part], BW), BW)],
+            raw.at[1 - slot, part], raw_send.at[slot, part], raw_recv.at[1 - slot, part],
+            beside(slot),
+        )
+
+    def raw_wait(slot, part):
+        remote(
+            raw.at[slot, part], raw.at[slot, part], raw_send.at[slot, part],
+            raw_recv.at[slot, part], sibling,
+        ).wait_recv()
+
+    def x_away():
+        return remote(xb0.at[core, chip], xn.at[other, chip], xz_send, xz_recv, beside(core))
+
+    def x_spread(k):
+        piece = xn.at[other, chip]
+        if k == 0:
+            return remote(piece, piece, fw_send.at[3, 0], fw_recv.at[3, 0], sibling)
+        return remote(
+            piece, piece, ag_send.at[3, k], ag_recv.at[3, k], (blk, mate(k) * 2 + core)
+        )
+
+    def x_hand(k):
+        piece = xn.at[other, source(k)]
+        return remote(piece, piece, fw_send.at[3, k], fw_recv.at[3, k], sibling)
+
+    def rs_copy(i, k, rs, rd):
+        return remote(
+            rs.at[mate(k)], rd.at[k], rs_send.at[i, k], rs_recv.at[i, k],
+            (blk, mate(k) * 2 + core),
+        )
+
+    def ag_copy(i, k, xb):
+        piece = xb.at[core, chip]
+        if k == 0:
+            return remote(piece, piece, fw_send.at[i, 0], fw_recv.at[i, 0], sibling)
+        return remote(
+            piece, piece, ag_send.at[i, k], ag_recv.at[i, k], (blk, mate(k) * 2 + core)
+        )
+
+    def scatter(i, ts, tr, rs, rd):
         core_copy(i, ts, tr).wait_recv()
         for k in FAR:
             rs[mate(k)] = ts[core, mate(k)] + tr[mate(k)]
-            copy = remote(
-                rs.at[mate(k)], rd.at[k], rs_send.at[i, k], rs_recv.at[i, k],
-                (blk, mate(k) * 2 + core),
-            )
-            copy.start()
-            pending.append(copy)
+            rs_copy(i, k, rs, rd).start()
+
+    def gather(i, ts, tr, rs, rd, xb, sign):
+        size = rs.shape[1] - 8
         total = ts[core, chip] + tr[chip]
         for k in FAR[::-1]:
-            remote(
-                rs.at[mate(k)], rd.at[k], rs_send.at[i, k], rs_recv.at[i, k],
-                (blk, mate(k) * 2 + core),
-            ).wait_recv()
+            rs_copy(i, k, rs, rd).wait_recv()
             total = total + rd[k]
         g = jnp.sum(
             jnp.where(eye(size, HB), jnp.broadcast_to(total[size : size + 1], (size, HB)), 0.0),
@@ -196,18 +255,8 @@
         )
         h = total[size + 1 : size + 2]
         xb[core, chip] = sign * total[:size] / (g + h + 1e-06)
-        for k in FAR:
-            copy = remote(
-                xb.at[core, chip], xb.at[core, chip], ag_send.at[i, k], ag_recv.at[i, k],
-                (blk, mate(k) * 2 + core),
-            )
-            copy.start()
-            pending.append(copy)
-        copy = remote(
-            xb.at[core, chip], xb.at[core, chip], fw_send.at[i, 0], fw_recv.at[i, 0], sibling
-        )
-        copy.start()
-        pending.append(copy)
+        for k in FAR + (0,):
+            ag_copy(i, k, xb).start()
 
     def hand_on(i, xb):
         for k in FAR[::-1]:
@@ -251,99 +300,137 @@
             copy = core_copy(0, ts0, tr0)
             copy.start()
             pending.append(copy)
+            for n in slots:
+
+                @pl.when(ahead(n))
+                def _(n=n):
+                    for p in range(2):
+                        raw_copy(n, p).start()
+
     sign = jnp.where((core == 0) & (blk > 0), 1.0, -1.0)
-    reduce_own(0, ts0, tr0, rs0, rd0, xb0, sign)
+    scatter(0, ts0, tr0, rs0, rd0)
+    gather(0, ts0, tr0, rs0, rd0, xb0, sign)
+
+    @pl.when(ahead(core))
+    def _():
+        x_away().start()
+
+    def spread():
+        piece = xn.at[other, chip]
+        remote(piece, piece, xz_send, xz_recv, sibling).wait_recv()
+        for k in FAR + (0,):
+            x_spread(k).start()
+
+    pl.when(ahead(other) & (is_relay | is_middle))(spread)
     hand_on(0, xb0)
 
-    half_rows = pin.shape[2] // 2
+    def rows_of(m):
+        return pl.ds(*pieces[m])
+
 
     def z_away(slot, column, m):
-        at = pl.ds(m * half_rows, half_rows)
+        at = rows_of(m)
         return remote(
             sb.at[slot, column, at], ra.at[1 - slot, column, at],
-            z_send.at[slot, column, m], z_recv.at[1 - slot, column, m],
-            (jnp.clip(blk + 2 * slot - 1, 0, last), rows),
+            z_send.at[slot, column, m], z_recv.at[1 - slot, column, m], beside(slot),
         )
 
     def z_here(slot, column, m):
-        at = pl.ds(m * half_rows, half_rows)
+        at = rows_of(m)
         return pltpu.make_async_copy(
             sb.at[slot, column, at], ra.at[slot, column, at], z_recv.at[slot, column, m]
         )
 
-    def at_edge(slot):
-        return blk == slot * last
+    def held(m):
+        return pl.ds(pieces[m][0] - direct, pieces[m][1])
+
+    def z_relay(slot, column, m):
+        return remote(
+            sb.at[slot, column, rows_of(m)], rl.at[column, held(m)],
+            z_send.at[slot, column, m], rl_recv.at[column, m], (last * slot, rows),
+        )
 
     def z_start(slot, column, m):
         @pl.when(at_edge(slot))
         def _():
             z_here(slot, column, m).start()
 
-        if m == 0:
-
-            @pl.when(jnp.logical_not(at_edge(slot)))
+        if kinds[m] < 2:
+
+            @pl.when(jnp.logical_not(at_edge(slot)) if kinds[m] == 0 else ahead(slot))
             def _():
                 z_away(slot, column, m).start()
 
-        else:
-
-            @pl.when(jnp.logical_not(at_edge(slot) | (blk == middle - slot)))
+        if kinds[m] > 0:
+
+            @pl.when(crosses(slot))
             def _():
-                z_away(slot, column, m).start()
-
-            @pl.when(blk == middle - slot)
-            def _():
-                remote(
-                    sb.at[slot, column, pl.ds(half_rows, half_rows)], rl.at[column],
-                    z_send.at[slot, column, 1], rl_recv.at[column], (last * slot, rows),
-                ).start()
-
-    def relay(column):
+                z_relay(slot, column, m).start()
+
+    def relay(column, m):
         goal = jnp.where(blk == last, 0, 1)
         return remote(
-            rl.at[column], ra.at[goal, column, pl.ds(half_rows, half_rows)],
-            rl_send.at[column], z_recv.at[goal, column, 1], (middle - goal, rows),
+            rl.at[column, held(m)], ra.at[goal, column, rows_of(m)],
+            rl_send.at[column, m], z_recv.at[goal, column, m], (middle - goal, rows),
         )
 
     def pass_on(column):
         @pl.when(is_relay)
         def _():
-            remote(
-                rl.at[column], rl.at[column], rl_send.at[column], rl_recv.at[column], sibling
-            ).wait_recv()
-            relay(column).start()
+            for m in (2, 3, 0, 1):
+                if kinds[m] == 0:
+                    continue
+                piece = rl.at[column, held(m)]
+                remote(
+                    piece, piece, rl_send.at[column, m], rl_recv.at[column, m], sibling
+                ).wait_recv()
+                relay(column, m).start()
 
     def z_wait_recv(slot, column, m):
-        at = pl.ds(m * half_rows, half_rows)
+        at = rows_of(m)
 
         @pl.when(at_edge(slot))
         def _():
             z_here(slot, column, m).wait()
 
-        @pl.when(jnp.logical_not(at_edge(slot)))
+        @pl.when(jnp.logical_not(at_edge(slot)) if kinds[m] < 2 else crosses(slot))
         def _():
             remote(
                 sb.at[slot, column, at], ra.at[slot, column, at],
                 z_send.at[slot, column, m], z_recv.at[slot, column, m], sibling,
             ).wait_recv()
 
+    def whole_x(xb, slot):
+        return jnp.concatenate(
+            [jnp.concatenate([xb[slot, 4 * p + n] for n in range(4)], axis=0) for p in range(2)],
+            axis=1,
+        )
+
+    def move(slot, m):
+        at = rows_of(m)
+        moved = turn(hl1[slot, at, :], w.at[slot], 0)
+        sb[slot, 0, at, :] = moved[:, :HB]
+        z_start(slot, 0, m)
+        sb[slot, 1, at, :] = moved[:, HB:]
+
+    def order(do, slot):
+        for m in (2, 3, 0, 1):
+            if kinds[m] == 2:
+                pl.when(jnp.logical_not(ahead(slot)))(functools.partial(do, m))
+            else:
+                do(m)
+
     for i, slot in enumerate((core, other)):
         if i == 1:
+
+            pl.when(ahead(other) & jnp.logical_not(is_relay | is_middle))(spread)
+
             receive_other(0, xb0)
-        x = jnp.concatenate(
-            [jnp.concatenate([xb0[slot, 4 * p + n] for n in range(4)], axis=0) for p in range(2)],
-            axis=1,
-        )
-        write_rotation(x, w.at[slot])
-        for m in range(2):
-            at = pl.ds(m * half_rows, half_rows)
-            moved = turn(hl1[slot, at, :], w.at[slot], 0)
-            sb[slot, 0, at, :] = moved[:, :HB]
-            z_start(slot, 0, m)
-            sb[slot, 1, at, :] = moved[:, HB:]
+        write_rotation(whole_x(xb0, slot), w.at[slot])
+        order(lambda m, slot=slot: move(slot, m), slot)
     for slot in (core, other):
-        for m in range(2):
-            z_start(slot, 1, m)
+        order(lambda m, slot=slot: z_start(slot, 1, m), slot)
+    half_rows = pin.shape[2] // 2
     for slot in (core, other):
         h = jnp.zeros((1, BW), F32)
         for m in range(2):
@@ -356,11 +443,40 @@
         hsum[1 - slot] = jnp.broadcast_to(h, (8, BW))
 
     pass_on(0)
+
+    @pl.when(ahead(other))
+    def _():
+        for k in FAR[::-1]:
+            piece = xn.at[other, source(k)]
+            remote(
+                piece, piece, ag_send.at[3, k], ag_recv.at[3, k], (blk, mate(k) * 2 + core)
+            ).wait_recv()
+            x_hand(k).start()
+
+    for i, slot in enumerate((other, core)):
+
+        @pl.when(ahead(slot))
+        def _(i=i, slot=slot):
+            if i == 1:
+                for k in (0,) + FAR[::-1]:
+                    piece = xn.at[core, source(k)]
+                    remote(
+                        piece, piece, fw_send.at[3, k], fw_recv.at[3, k], sibling
+                    ).wait_recv()
+            write_rotation(whole_x(xn, slot), w.at[slot])
+            for p in range(2):
+                raw_wait(slot, p)
+            ah, al = split(raw[slot, 0])
+            bh, bl = split(raw[slot, 1])
+            turned = turn(jnp.concatenate([ah, bh, al, bl], axis=1), w.at[slot], 0)
+            ra[slot, 0, tail, :] = turned[:, :HB]
+            ra[slot, 1, tail, :] = turned[:, HB:]
+
     sign = jnp.where(core == 0, -1.0, 1.0)
     second = ((ts1, tr1, rs1, rd1, xb1), (ts2, tr2, rs2, rd2, xb2))
     for column, (ts, tr, rs, rd, xb) in enumerate(second):
         for i, slot in enumerate(slots):
-            for m in range(2):
+            for m in range(count):
                 z_wait_recv(slot, column, m)
 
             def part(n, g, slot=slot, column=column):
@@ -383,12 +499,23 @@
                 copy.start()
                 pending.append(copy)
         if column == 0:
+            scatter(1, ts, tr, rs, rd)
             pass_on(1)
-        if column == 1:
-            whole = pltpu.make_async_copy(hl2, hl_out, out_sem.at[0])
-            whole.start()
-            hand_on(1, xb1)
-        reduce_own(1 + column, ts, tr, rs, rd, xb, sign)
+
+            @pl.when(jnp.logical_not(late))
+            def _():
+                gather(1, *second[0], sign)
+
+    whole = pltpu.make_async_copy(hl2, hl_out, out_sem.at[0])
+    whole.start()
+
+    @pl.when(late)
+    def _():
+        gather(1, *second[0], sign)
+
+    scatter(2, *second[1][:4])
+    hand_on(1, xb1)
+    gather(2, *second[1], sign)
     hand_on(2, xb2)
     outs = []
     for column, xb in enumerate((xb1, xb2)):
@@ -398,18 +525,52 @@
         outs.append(copy)
     for copy in pending:
         copy.wait_send()
+    for i, (rs, rd, xb) in enumerate(((rs0, rd0, xb0), (rs1, rd1, xb1), (rs2, rd2, xb2))):
+        for k in FAR:
+            rs_copy(i, k, rs, rd).wait_send()
+        for k in FAR + (0,):
+            ag_copy(i, k, xb).wait_send()
     for slot in range(2):
+
+        @pl.when(jnp.logical_not(at_edge(slot)))
+        def _(slot=slot):
+            for column in range(2):
+                for m in range(count):
+                    if kinds[m] == 0:
+                        z_away(slot, column, m).wait_send()
+
+        @pl.when(crosses(slot))
+        def _(slot=slot):
+            for column in range(2):
+                for m in range(count):
+                    if kinds[m] > 0:
+                        z_relay(slot, column, m).wait_send()
+
+        @pl.when(ahead(slot))
+        def _(slot=slot):
+            for p in range(2):
+                for m in range(count):
+                    if kinds[m] == 1:
+                        z_away(slot, p, m).wait_send()
+                raw_copy(slot, p).wait_send()
+
+    @pl.when(ahead(core))
+    def _():
+        x_away().wait_send()
+
+    @pl.when(ahead(other))
+    def _():
+        for k in FAR + (0,):
+            x_spread(k).wait_send()
+        for k in FAR:
+            x_hand(k).wait_send()
+
+    @pl.when(is_relay)
+    def _():
         for column in range(2):
-            for m in range(2):
-
-                @pl.when(jnp.logical_not(at_edge(slot)))
-                def _():
-                    z_away(slot, column, m).wait_send()
-
-    @pl.when(is_relay)
-    def _():
-        for column in range(2):
-            relay(column).wait_send()
+            for m in range(count):
+                if kinds[m] > 0:
+                    relay(column, m).wait_send()
 
     whole.wait()
     for copy in outs:
@@ -484,7 +645,9 @@
             pltpu.VMEM((2, 4 * BW, 2 * BW), BF16),
             pltpu.VMEM((2, 2, rows, HB), F32),
             pltpu.VMEM((2, 2, rows, HB), F32),
-            pltpu.VMEM((2, rows // 2, HB), F32),
+            pltpu.VMEM((2, rows - sum(s for s, k in zip((320, 320, 128, 256), (0, 0, 1, 2)) if k == 0), HB), F32),
+            pltpu.VMEM((2, 2, 256, BW), F32),
+            pltpu.VMEM((2, 8, 64, HB), F32),
             pltpu.VMEM((2, 8, BW), F32),
             *per_step(lambda size: pltpu.VMEM((2, 8, size + 8, HB), F32)),
             *per_step(lambda size: pltpu.VMEM((8, size + 8, HB), F32)),
@@ -497,14 +660,18 @@
             dma((3,)),
             dma((3, 8)),
             dma((3, 8)),
-            dma((3, 8)),
-            dma((3, 8)),
-            dma((3, 8)),
-            dma((3, 8)),
-            dma((2, 2, 2)),
-            dma((2, 2, 2)),
-            dma((2,)),
-            dma((2,)),
+            dma((4, 8)),
+            dma((4, 8)),
+            dma((4, 8)),
+            dma((4, 8)),
+            dma((2, 2, 8)),
+            dma((2, 2, 8)),
+            dma((2, 8)),
+            dma((2, 8)),
+            dma((2, 2)),
+            dma((2, 2)),
+            dma,
+            dma,
         ],
         compiler_params=pltpu.CompilerParams(
             collective_id=0, has_side_effects=True, vmem_limit_bytes=48 * 2**20

time: 68.7 us -> 64.5 us (0.939)
  the two profiles are of different devices: /device:TPU:17 before, /device:TPU:1 now
where the time goes in v2:
time: 64.5 us; the launch traced here: 64.4 us
  Pallas kernels  64.3 us (100%)
    pallas_call x1, Pallas kernels, local(): pl.pallas_call(jacobi, out_shape=(jax.ShapeDtypeStruct((2, rows, 4 * BW),...  57.7 us
    pallas_call x1, Pallas kernels, local(): pl.pallas_call(finish, out_shape=jax.ShapeDtypeStruct(operator.shape, F32...  6.62 us

profile of v2, /device:TPU:1, one launch (start us, length us, event | category | flops | bytes accessed | tf_op | source)
XLA Modules:
  0.0 64.4 jit_solution(2158838396982928643)
XLA Ops:
  0.0 57.7 %jacobi.1 = (bf16[2,1024,1024]{2,1,0:T(8,128)(2,1)S(1)}, f32[2,2,8,32,128]{4,3,2,1,0:T(8,128)S(1)}) custom-call(f32[1024,1024]{1,0:T(8,128)} %op.1), custom_call_target="tpu_custom_call" | custom-call | tf_op jit(solution)/shard_map/jacobi/pallas_call | solution.py:633
  57.7 6.6 %finish.1 = f32[1024,1024]{1,0:T(8,128)} custom-call(bf16[2,1024,1024]{2,1,0:T(8,128)(2,1)S(1)} %get-tuple-element.7.hl_in, f32[2,2,8,32,128]{4,3,2,1,0:T(8,128)S(1)} %get-tuple-element.8.x_in), custom_call_target="tpu_custom_call" | custom-call | tf_op jit(solution)/shard_map/finish/pallas_call | solution.py:681

commit v3 on v2

--- a/solution.py
+++ b/solution.py
@@ -591,7 +591,8 @@
             )
             loads[slot, m].start()
     x_copy.wait()
-    stores = []
+    for load in loads.values():
+        load.wait()
     for slot in range(2):
         x = jnp.concatenate(
             [
@@ -603,9 +604,10 @@
             axis=1,
         )
         write_rotation(x, w.at[slot])
+    stores = []
+    for slot in range(2):
         for m in range(count):
             at = pl.ds(m * size, size)
-            loads[slot, m].wait()
             lhs = hl[slot, at, :]
             first = slot * 2 * BW
             for p in range(2):

time: 64.5 us -> 63.4 us (0.983)
  Pallas kernels: 64.3 us -> 63.2 us
    pallas_call x1, Pallas kernels: 6.62 us -> 5.54 us  [local(): pl.pallas_call(finish, out_shape=jax.ShapeDtypeStruct(operator.shape, F32...]
where the time goes in v3:
time: 63.4 us
  Pallas kernels  63.2 us (100%)
    pallas_call x1, Pallas kernels, local(): pl.pallas_call(jacobi, out_shape=(jax.ShapeDtypeStruct((2, rows, 4 * BW),...  57.7 us
    pallas_call x1, Pallas kernels, local(): pl.pallas_call(finish, out_shape=jax.ShapeDtypeStruct(operator.shape, F32...  5.54 us

profile of v3, /device:TPU:1, one launch (start us, length us, event | category | flops | bytes accessed | tf_op | source)
XLA Modules:
  0.0 63.4 jit_solution(2923984142673055312)
XLA Ops:
  0.0 57.7 %jacobi.1 = (bf16[2,1024,1024]{2,1,0:T(8,128)(2,1)S(1)}, f32[2,2,8,32,128]{4,3,2,1,0:T(8,128)S(1)}) custom-call(f32[1024,1024]{1,0:T(8,128)} %op.1), custom_call_target="tpu_custom_call" | custom-call | tf_op jit(solution)/shard_map/jacobi/pallas_call | solution.py:635
  57.7 5.5 %finish.1 = f32[1024,1024]{1,0:T(8,128)} custom-call(bf16[2,1024,1024]{2,1,0:T(8,128)(2,1)S(1)} %get-tuple-element.7.hl_in, f32[2,2,8,32,128]{4,3,2,1,0:T(8,128)S(1)} %get-tuple-element.8.x_in), custom_call_target="tpu_custom_call" | custom-call | tf_op jit(solution)/shard_map/finish/pallas_call | solution.py:683

commit v4 on v3

--- a/solution.py
+++ b/solution.py
@@ -516,20 +516,19 @@
     scatter(2, *second[1][:4])
     hand_on(1, xb1)
     gather(2, *second[1], sign)
-    hand_on(2, xb2)
-    outs = []
-    for column, xb in enumerate((xb1, xb2)):
-        receive_other(1 + column, xb)
-        copy = pltpu.make_async_copy(xb, x_out.at[column], out_sem.at[1 + column])
-        copy.start()
-        outs.append(copy)
+    receive_other(1, xb1)
+    outs = [pltpu.make_async_copy(xb1, x_out.at[0], out_sem.at[1])]
+    outs[0].start()
+
     for copy in pending:
         copy.wait_send()
+    pending.clear()
     for i, (rs, rd, xb) in enumerate(((rs0, rd0, xb0), (rs1, rd1, xb1), (rs2, rd2, xb2))):
         for k in FAR:
             rs_copy(i, k, rs, rd).wait_send()
-        for k in FAR + (0,):
-            ag_copy(i, k, xb).wait_send()
+        if i < 2:
+            for k in FAR + (0,):
+                ag_copy(i, k, xb).wait_send()
     for slot in range(2):
 
         @pl.when(jnp.logical_not(at_edge(slot)))
@@ -573,6 +572,14 @@
                     relay(column, m).wait_send()
 
     whole.wait()
+    hand_on(2, xb2)
+    receive_other(2, xb2)
+    outs.append(pltpu.make_async_copy(xb2, x_out.at[1], out_sem.at[2]))
+    outs[1].start()
+    for copy in pending:
+        copy.wait_send()
+    for k in FAR + (0,):
+        ag_copy(2, k, xb2).wait_send()
     for copy in outs:
         copy.wait()
 

time: 63.4 us -> 63.3 us (level)
  no operation moved by 1% of the time
where the time goes in v4:
time: 63.3 us; the launch traced here: 63.2 us
  Pallas kernels  63.1 us (100%)
    pallas_call x1, Pallas kernels, local(): pl.pallas_call(jacobi, out_shape=(jax.ShapeDtypeStruct((2, rows, 4 * BW),...  57.5 us
    pallas_call x1, Pallas kernels, local(): pl.pallas_call(finish, out_shape=jax.ShapeDtypeStruct(operator.shape, F32...  5.54 us

profile of v4, /device:TPU:1, one launch (start us, length us, event | category | flops | bytes accessed | tf_op | source)
XLA Modules:
  0.0 63.2 jit_solution(12915806941977941001)
XLA Ops:
  0.0 57.5 %jacobi.1 = (bf16[2,1024,1024]{2,1,0:T(8,128)(2,1)S(1)}, f32[2,2,8,32,128]{4,3,2,1,0:T(8,128)S(1)}) custom-call(f32[1024,1024]{1,0:T(8,128)} %op.1), custom_call_target="tpu_custom_call" | custom-call | tf_op jit(solution)/shard_map/jacobi/pallas_call | solution.py:642
  57.5 5.5 %finish.1 = f32[1024,1024]{1,0:T(8,128)} custom-call(bf16[2,1024,1024]{2,1,0:T(8,128)(2,1)S(1)} %get-tuple-element.7.hl_in, f32[2,2,8,32,128]{4,3,2,1,0:T(8,128)S(1)} %get-tuple-element.8.x_in), custom_call_target="tpu_custom_call" | custom-call | tf_op jit(solution)/shard_map/finish/pallas_call | solution.py:690
